TPU v7x, 32 devices: a whole 2x2x4 slice. The times are simulated.
32 devices in a mesh: frame: 16 (over z, x, core), row: 2 (over y).
Axes of the slice: x: 2, y: 2, z: 4, core: 2. Of those that a mesh axis runs over, the one named last changes fastest.
Arguments:
- latents: bfloat16 [64, 32, 32, 320], P('frame', 'row'), may hold values from -20 to 20
- ln_gain: bfloat16 [320], replicated, may hold values from 0.099609375 to 1.8984375
- q_weight: bfloat16 [320, 320], replicated, may hold values from -0.30078125 to 0.30078125
- k_weight: bfloat16 [320, 320], replicated, may hold values from -3 to 3
- v_weight: bfloat16 [320, 320], replicated, may hold values from -0.3125 to 0.3125
- o_weight: bfloat16 [320, 320], replicated, may hold values from -0.3125 to 0.3125
- gn_gain: bfloat16 [320], replicated, may hold values from 0.099609375 to 1.8984375
- conv_weight: bfloat16 [3, 3, 320, 320], replicated, may hold values from -0.109375 to 0.109375
- conv_bias: bfloat16 [320], replicated, may hold values from -3 to 3
Outputs:
- output: bfloat16 [64, 32, 32, 320], P('frame', 'row')
All inputs are finite; a program needn't handle non-finite values.
Results may differ from a plain program's by a relative error of at most 0.0085.
The roundings to bfloat16 on the way count: a program that leaves them out, or rounds other values in their place, can miss the bound.
Values may be sent and summed in bfloat16 or wider, within the bound.
No kernel may reach another device: no remote copies, remote signals or barrier semaphores. Data moves between devices by JAX's collectives and lax.ppermute only.
A program may use at most 128 MiB of HBM per device.

v0:
```python
import functools
import math

import jax
import jax.numpy as jnp
from jax import lax
from jax.experimental import pallas as pl
from jax.experimental.pallas import tpu as pltpu
from jax.sharding import PartitionSpec as P

HEADS = 8
GROUPS = 32
KPAD = 64
VPAD = 48
BF16, F32, I32 = jnp.bfloat16, jnp.float32, jnp.int32
VMEM_BYTES = 24 * 2**20
LOW = -1e30


def dot(a, b):
    return jnp.dot(a, b, preferred_element_type=F32)


def nt(a, b):
    return lax.dot_general(a, b, (((1,), (1,)), ((), ())), preferred_element_type=F32)


def tn(a, b):
    return lax.dot_general(a, b, (((0,), (0,)), ((), ())), preferred_element_type=F32)


def cost(flops, moved, exps=0):
    return pl.CostEstimate(flops=int(flops), bytes_accessed=int(moved), transcendentals=int(exps))


def near_of(*dims, dtype=BF16):
    return pltpu.VMEM(dims, dtype)


def far_of(*dims, dtype=BF16):
    return pltpu.HBM(dims, dtype)


def near(a):
    return pltpu.with_memory_space_constraint(a, pltpu.VMEM)


def far(a):
    return pltpu.with_memory_space_constraint(a, pltpu.HBM)


def kernel_call(body, name, near_args, far_args, outs, scratch, price, aliases=None):
    in_vmem, anywhere = pl.BlockSpec(memory_space=pltpu.VMEM), pl.BlockSpec(memory_space=pl.ANY)
    return pl.pallas_call(
        body,
        in_specs=[in_vmem] * len(near_args) + [anywhere] * len(far_args),
        out_specs=[in_vmem if o.memory_space == pltpu.VMEM else anywhere for o in outs],
        out_shape=outs,
        scratch_shapes=scratch,
        input_output_aliases=aliases or {},
        compiler_params=pltpu.CompilerParams(vmem_limit_bytes=VMEM_BYTES),
        cost_estimate=price,
        name=name,
    )(*[near(a) for a in near_args], *[far(a) for a in far_args])


def head_spread(channels, pad):
    dim = channels // HEADS
    shape = (HEADS * pad, channels)
    row = lax.broadcasted_iota(I32, shape, 0)
    col = lax.broadcasted_iota(I32, shape, 1)
    head = sum((row >= h * pad).astype(I32) for h in range(1, HEADS))
    inside = row - head * pad
    return jnp.where((inside < dim) & (head * dim + inside == col), 1.0, 0.0).astype(BF16)


def project_kernel(x_hbm, g_hbm, wq_hbm, wk_hbm, wv_hbm, wo_hbm,
                   qt_ref, main_hbm, first_ref, last_ref, wkp_ref, wvt_ref, wop_ref,
                   x_ref, g_ref, w_ref, main_ref, x_sem, w_sem, main_sem):
    frames, tok, ch = x_ref.shape
    copies = [pltpu.make_async_copy(g_hbm, g_ref, w_sem.at[4])]
    copies += [pltpu.make_async_copy(x_hbm.at[f], x_ref.at[f], x_sem.at[f]) for f in range(frames)]
    weights = [pltpu.make_async_copy(w, w_ref.at[k], w_sem.at[k])
               for k, w in enumerate((wq_hbm, wk_hbm, wv_hbm, wo_hbm))]
    for copy in copies + weights:
        copy.start()
    ek, ev = head_spread(ch, KPAD), head_spread(ch, VPAD)
    copies[0].wait()
    gain = jnp.broadcast_to(g_ref[...].astype(F32).reshape(1, ch), (8, ch)).T[:, 0:1]

    def normed(f):
        copies[1 + f].wait()
        floated = x_ref[f].astype(F32).T
        centre = floated - jnp.sum(floated, axis=0, keepdims=True) / ch
        spread = jnp.sum(centre * centre, axis=0, keepdims=True) / ch
        return (centre * lax.rsqrt(spread + 1e-05) * gain).astype(BF16)

    leave = []
    for f in range(frames):
        value = normed(f)
        if f < frames - 1:
            main_ref[f] = value
            leave.append(pltpu.make_async_copy(main_ref.at[f], main_hbm.at[f], main_sem.at[f]))
            leave[-1].start()
        else:
            last_ref[0] = value
        if f == 0:
            first_ref[0] = value
            for copy in weights:
                copy.wait()
            wqt = nt(ek, w_ref[0]).astype(BF16)
            wkp_ref[...] = nt(w_ref[1], ek).astype(BF16)
            wvt_ref[...] = nt(ev, w_ref[2]).astype(BF16)
            wop_ref[...] = dot(ev, w_ref[3]).astype(BF16)
        qt_ref[f] = dot(wqt, value).astype(BF16)
    for copy in leave:
        copy.wait()


def project(x, gain, wq, wk, wv, wo):
    frames, tok, ch = x.shape
    nk, nv = HEADS * KPAD, HEADS * VPAD
    outs = [near_of(frames, nk, tok), far_of(frames - 1, ch, tok), near_of(1, ch, tok), near_of(1, ch, tok),
            near_of(ch, nk), near_of(nv, ch), near_of(nv, ch)]
    scratch = [pltpu.VMEM(x.shape, BF16), pltpu.VMEM((ch,), BF16), pltpu.VMEM((4, ch, ch), BF16),
               pltpu.VMEM((frames - 1, ch, tok), BF16), pltpu.SemaphoreType.DMA((frames,)),
               pltpu.SemaphoreType.DMA((5,)), pltpu.SemaphoreType.DMA((frames - 1,))]
    return kernel_call(project_kernel, "project", [], [x, gain, wq, wk, wv, wo], outs, scratch,
                       cost(frames * tok * ch * nk, 8e5))


class Flash:
    def __init__(self, qt_ref, wkp_ref, wvt_ref, state_in, state_out, scratch):
        self.qt, self.wkp, self.wvt = qt_ref, wkp_ref, wvt_ref
        self.state_in, self.state_out = state_in, state_out
        self.acc, self.s, self.in_sem, self.out_sem, *kept = scratch
        if kept:
            self.k, self.vt = kept
        self.tok = qt_ref.shape[2]
        self.dim = wkp_ref.shape[0] // HEADS
        self.factor = math.log2(math.e) / math.sqrt(self.dim)

    def in_copy(self, f):
        return pltpu.make_async_copy(self.state_in.at[f], self.acc.at[f], self.in_sem.at[f])

    def out_copy(self, f):
        return pltpu.make_async_copy(self.acc.at[f], self.state_out.at[f], self.out_sem.at[f])

    def part_copy(self, f, h):
        rows = pl.ds((h - 1) * VPAD, 2 * VPAD)
        return pltpu.make_async_copy(self.acc.at[f, rows], self.state_out.at[f, rows], self.out_sem.at[f])

    def make_keys(self, seg):
        self.k[0:seg.shape[1], :] = tn(seg, self.wkp[...]).astype(BF16)

    def make_values(self, seg):
        keys = seg.shape[1]
        ones_row = lax.broadcasted_iota(I32, (16, keys), 0) == self.dim % 16
        vt = dot(self.wvt[...], seg).astype(BF16)
        for h in range(HEADS):
            at, end = h * VPAD + self.dim // 16 * 16, (h + 1) * VPAD
            self.vt[h * VPAD:at, 0:keys] = vt[h * VPAD:at]
            self.vt[at:at + 16, 0:keys] = jnp.where(ones_row, jnp.ones((16, keys), BF16), vt[at:at + 16])
            if at + 16 < end:
                self.vt[at + 16:end, 0:keys] = vt[at + 16:end]

    def scores(self, f, h, keys):
        own = self.qt[f, h * KPAD:(h + 1) * KPAD, :]
        zeros = jnp.zeros((KPAD, self.tok), BF16)
        both = jnp.concatenate([own, zeros] if h % 2 == 0 else [zeros, own], axis=0)
        lanes = h // 2 * 2 * KPAD
        self.s[h % 2, 0:keys] = dot(self.k[0:keys, lanes:lanes + 2 * KPAD], both)

    def begin(self, f, seg):
        self.make_keys(seg)
        self.make_values(seg)
        self.scores(f, 0, seg.shape[1])

    def item(self, f, keys, after=None, seg=None, first=False, attended=None, leave=False):
        for h in range(HEADS):
            top = jnp.max(self.s[h % 2, 0:keys], axis=0, keepdims=True)
            if h + 1 < HEADS:
                self.scores(f, h + 1, keys)
            elif after is not None:
                if seg is not None:
                    self.make_keys(seg)
                self.scores(after, 0, keys if seg is None else seg.shape[1])
            rows = slice(h * VPAD, (h + 1) * VPAD)
            if not first:
                kept = self.acc[f, rows, :]
                old = kept[self.dim + 1:self.dim + 2]
                top = jnp.maximum(top, old)
            weights = jnp.exp2((self.s[h % 2, 0:keys] - top) * self.factor).astype(BF16)
            part = dot(self.vt[rows, 0:keys], weights)
            if not first:
                part = part + kept * jnp.exp2((old - top) * self.factor)
            if attended is not None:
                attended[rows, :] = (part / part[self.dim:self.dim + 1]).astype(BF16)
            else:
                self.acc[f, rows, :] = part
                self.acc[f, h * VPAD + self.dim + 1:h * VPAD + self.dim + 2, :] = top
                if leave and h % 2 == 1:
                    self.part_copy(f, h).start()
        if after is not None and seg is not None:
            self.make_values(seg)


class Arriving:
    def __init__(self, hbm, near_ref, sem, start=0):
        self.hbm, self.near, self.sem = hbm, near_ref, sem
        for k in range(start, hbm.shape[0]):
            self.copy(k).start()

    def copy(self, k):
        return pltpu.make_async_copy(self.hbm.at[k], self.near.at[k], self.sem.at[k])

    def __getitem__(self, k):
        self.copy(k).wait()
        return self.near[k]


def own_kernel(qt_ref, wkp_ref, wvt_ref, first_ref, main_hbm, state_out, main_near, main_sem, *scratch):
    flash = Flash(qt_ref, wkp_ref, wvt_ref, None, state_out, scratch)
    frames, keys = qt_ref.shape[0], main_hbm.shape[2]
    main = Arriving(main_hbm, main_near, main_sem, 1)
    flash.begin(1, first_ref[0])

    @pl.loop(1, frames - 1)
    def _(f):
        flash.item(f, keys, f + 1, main[f], first=True)
        flash.out_copy(f).start()

    flash.item(frames - 1, keys, first=True, leave=True)
    for f in range(1, frames):
        flash.out_copy(f).wait()


def side_kernel(qt_ref, wkp_ref, wvt_ref, prev_ref, first_ref, side_hbm, state_in, state_out, mirror_ref,
                side_near, side_sem, *scratch):
    flash = Flash(qt_ref, wkp_ref, wvt_ref, state_in, state_out, scratch)
    frames, keys = qt_ref.shape[0], side_hbm.shape[2]
    side = Arriving(side_hbm, side_near, side_sem)
    for f in range(1, frames):
        flash.in_copy(f).start()
    flash.begin(0, jnp.where(lax.axis_index("frame") > 0, prev_ref[0], first_ref[0]))
    leading = side[0]
    mirror_ref[0] = leading
    flash.item(0, prev_ref.shape[2], 1, leading, first=True)
    flash.out_copy(0).start()

    @pl.loop(1, frames - 1)
    def _(f):
        flash.in_copy(f).wait()
        flash.item(f, keys, f + 1, side[f])
        flash.out_copy(f).start()

    flash.in_copy(frames - 1).wait()
    flash.item(frames - 1, keys, leave=True)
    for f in range(frames):
        flash.out_copy(f).wait()


def lead_kernel(qt_ref, wkp_ref, wvt_ref, prev_ref, mirror_ref, lead_ref, state_in, state_out, *scratch):
    flash = Flash(qt_ref, wkp_ref, wvt_ref, state_in, state_out, scratch)
    frames, keys = qt_ref.shape[0], lead_ref.shape[2]
    for f in range(frames):
        flash.in_copy(f).start()
    flash.begin(0, jnp.where(lax.axis_index("frame") > 0, prev_ref[0], mirror_ref[0]))
    flash.in_copy(0).wait()
    flash.item(0, prev_ref.shape[2], 0, lead_ref[0])
    flash.item(0, keys, 1)
    flash.out_copy(0).start()

    @pl.loop(1, frames - 1)
    def _(f):
        flash.in_copy(f).wait()
        flash.item(f, keys, f + 1)
        flash.out_copy(f).start()

    flash.in_copy(frames - 1).wait()
    flash.item(frames - 1, keys, leave=True)
    for f in range(frames):
        flash.out_copy(f).wait()


def finish_kernel(start, rows, pair, fresh, *refs):
    refs = list(refs)
    take = lambda n: [refs.pop(0) for _ in range(n)]
    qt_ref, wkp_ref, wvt_ref, wop_ref = take(4)
    if fresh:
        (seg_ref,) = take(1)
    else:
        k_ref, vt_ref = take(2)
    state_hbm, x_hbm, upd_ref, edge_ref, stat_ref = take(5)
    if fresh:
        k_ref, vt_ref = take(2)
    att_ref, x_ref, x_sem = take(3)
    count, tok, ch = x_ref.shape
    cols, keys = tok // rows, k_ref.shape[0]
    flash = Flash(qt_ref, wkp_ref, wvt_ref, state_hbm, None, refs)
    flash.k, flash.vt = k_ref, vt_ref
    for f in range(start, start + count):
        flash.in_copy(f).start()
    copy = pltpu.make_async_copy(x_hbm.at[pl.ds(start, count)], x_ref, x_sem)
    copy.start()
    if fresh:
        flash.begin(start, seg_ref[0])
    else:
        flash.scores(start, 0, keys)

    @pl.loop(0, count)
    def _(i):
        flash.in_copy(start + i).wait()
        flash.item(start + i, keys, start + jnp.minimum(i + 1, count - 1), attended=att_ref)

        @pl.when(i == 0)
        def _():
            copy.wait()

        mixed = tn(att_ref[...], wop_ref[...])
        updated = (x_ref[i].astype(F32) + mixed).astype(BF16)
        upd_ref[i] = updated
        floated = updated.astype(F32)
        sums = jnp.sum(floated, axis=0, keepdims=True)
        squares = jnp.sum(floated * floated, axis=0, keepdims=True)
        which = lax.broadcasted_iota(I32, (8, ch), 0)
        stats = jnp.where(which == 0, sums, jnp.where(which == 1, squares, 0.0))
        stat_ref[i] = stats
        if pair:
            edge_ref[i, 0:cols] = jnp.where(lax.axis_index("row") == 0, floated[tok - cols:], floated[:cols])
            edge_ref[i, cols:cols + 8] = stats
        else:
            edge_ref[i, 0:cols] = floated[:cols]
            edge_ref[i, cols:2 * cols] = floated[tok - cols:]


def flash_scratch(qt, keys, held=True):
    frames, nk, tok = qt.shape
    nv = HEADS * VPAD
    out = [pltpu.VMEM((frames, nv, tok), F32), pltpu.VMEM((2, keys, tok), F32)]
    out += [pltpu.SemaphoreType.DMA((frames,))] * 2
    return out + ([pltpu.VMEM((keys, nk), BF16), pltpu.VMEM((nv, keys), BF16)] if held else [])


def flash_cost(items, keys, tok):
    made = items * HEADS * keys * tok
    return cost(made * 140, made // 80, made // 10)


def flash(body, name, qt, wkp, wvt, segments, state, items, moved=None, mirrored=False):
    frames, _, tok = qt.shape
    keys = max(s.shape[2] for s in segments + ([] if moved is None else [moved]))
    near_args, far_args, scratch = [qt, wkp, wvt] + segments, [], []
    if moved is not None:
        far_args.append(moved)
        scratch = [pltpu.VMEM(moved.shape, BF16), pltpu.SemaphoreType.DMA((moved.shape[0],))]
    aliases = {}
    if state is not None:
        far_args.append(state)
        aliases = {len(near_args) + len(far_args) - 1: 0}
    outs = [far_of(frames, HEADS * VPAD, tok, dtype=F32)] + ([near_of(1, *moved.shape[1:])] if mirrored else [])
    got = kernel_call(body, name, near_args, far_args, outs, scratch + flash_scratch(qt, keys),
                      flash_cost(items, keys, tok), aliases)
    return got if mirrored else got[0]


def finish(start, count, qt, wkp, wvt, wop, state, lead_side, made, x, rows, pair):
    tok, ch = x.shape[1:]
    cols, nk, nv, keys = tok // rows, HEADS * KPAD, HEADS * VPAD, lead_side.shape[2]
    fresh = made is None
    outs = [near_of(count, tok, ch), near_of(count, cols + 8 if pair else 2 * cols, ch, dtype=F32),
            near_of(count, 8, ch, dtype=F32)]
    if fresh:
        outs += [near_of(keys, nk), near_of(nv, keys)]
    scratch = [pltpu.VMEM((nv, tok), BF16), pltpu.VMEM((count, tok, ch), BF16), pltpu.SemaphoreType.DMA]
    got = kernel_call(functools.partial(finish_kernel, start, rows, pair, fresh), "finish",
                      [qt, wkp, wvt, wop] + ([lead_side] if fresh else list(made)), [state, x], outs,
                      scratch + flash_scratch(qt, keys, held=False), flash_cost(count, keys, tok))
    return got[:3], (tuple(got[3:]) if fresh else made)


def conv_kernel(start, rows, counted, pair, fresh, *refs):
    refs = list(refs)
    take = lambda n: [refs.pop(0) for _ in range(n)]
    upd_ref, top_ref, bot_ref, stat_ref, gn_ref, bias_ref, w_ref = take(7)
    if not fresh:
        take(1)
    (out_hbm,) = take(1)
    if fresh:
        (wide_ref,) = take(1)
    act_ref, out_ref, sems = refs
    count, tok, ch = upd_ref.shape
    cols = tok // rows
    if fresh:
        for a in range(3):
            for b in range(3):
                wide_ref[a * ch:(a + 1) * ch, b * ch:(b + 1) * ch] = w_ref[a, b]
    else:
        wide_ref = w_ref

    stats = jnp.concatenate([stat_ref[i] + top_ref[i, cols:cols + 8] if pair else stat_ref[i]
                             for i in range(count)], axis=0)
    width = ch // GROUPS
    first = lax.broadcasted_iota(I32, (ch, ch), 0)
    second = lax.broadcasted_iota(I32, (ch, ch), 1)
    group_of = lambda v: (v * (65536 // width + 1)) >> 16
    same = jnp.where(group_of(first) == group_of(second), 1.0, 0.0).astype(BF16)
    high = stats.astype(BF16)
    rest = stats - high.astype(F32)
    middle = rest.astype(BF16)
    low = (rest - middle.astype(F32)).astype(BF16)
    grouped = (dot(high, same) + dot(middle, same) + dot(low, same)) / counted
    gain = gn_ref[...].astype(F32).reshape(1, ch)
    bias = bias_ref[...].astype(F32).reshape(1, ch)
    me = lax.axis_index("row")
    column = lax.broadcasted_iota(I32, (tok, ch), 0) % cols
    copies = []
    for i in range(count):
        mean = grouped[8 * i:8 * i + 1]
        scale = lax.rsqrt(grouped[8 * i + 1:8 * i + 2] - mean * mean + 1e-05) * gain

        def activated(u):
            v = (u.astype(F32) - mean) * scale
            return (v / (1.0 + jnp.exp(-v))).astype(BF16)

        above = jnp.where(me > 0, activated(top_ref[i, 0:cols]), jnp.zeros((cols, ch), BF16))
        below = jnp.where(me < lax.axis_size("row") - 1, activated(bot_ref[i, 0:cols]), jnp.zeros((cols, ch), BF16))
        inner = activated(upd_ref[i])
        act_ref[:, ch:2 * ch] = inner
        act_ref[0:cols, 0:ch] = above
        act_ref[cols:tok, 0:ch] = inner[0:tok - cols]
        act_ref[0:tok - cols, 2 * ch:] = inner[cols:tok]
        act_ref[tok - cols:tok, 2 * ch:] = below
        parts = dot(act_ref[...], wide_ref[...])
        left = jnp.where(column == 0, 0.0, pltpu.roll(parts[:, 0:ch], 1, 0))
        right = jnp.where(column == cols - 1, 0.0, pltpu.roll(parts[:, 2 * ch:], tok - 1, 0))
        out_ref[i] = (upd_ref[i].astype(F32) + (left + parts[:, ch:2 * ch] + right) + bias).astype(BF16)
        copies.append(pltpu.make_async_copy(out_ref.at[i], out_hbm.at[start + i], sems.at[i]))
        copies[-1].start()
    for copy in copies:
        copy.wait()


def conv(start, frames, upd, top, bot, stats, gn, bias, weight, rows, pair, counted, into=None):
    count, tok, ch = upd.shape
    fresh = into is None
    args = [upd, top, bot, stats, gn, bias, weight if fresh else into[1]]
    outs = [far_of(frames, tok, ch)] + ([near_of(3 * ch, 3 * ch)] if fresh else [])
    scratch = [pltpu.VMEM((tok, 3 * ch), BF16), pltpu.VMEM((count, tok, ch), BF16),
               pltpu.SemaphoreType.DMA((count,))]
    got = kernel_call(functools.partial(conv_kernel, start, rows, counted, pair, fresh), "conv",
                      args, [] if fresh else [into[0]], outs, scratch, cost(count * tok * ch * ch * 30, 4e6),
                      {} if fresh else {len(args): 0})
    return got[0], got[1] if fresh else into[1]


def fan(value, axis, heads, steps):
    size = lax.axis_size(axis)
    got = {}
    for k in steps:
        route = [(i, i + k) for i in heads if i + k < size]
        if route:
            got[k] = lax.ppermute(value, axis, route)
    return got


def chosen_kernel(axis, modulus, places, *refs):
    place = lax.axis_index(axis) % modulus
    *sources, out_hbm, sem = refs
    elsewhere = place >= 0
    for k, source in zip(places, sources[1:]):
        here = place == k
        elsewhere = elsewhere & (place != k)

        @pl.when(here)
        def _(source=source):
            copy = pltpu.make_async_copy(source, out_hbm, sem)
            copy.start()
            copy.wait()

    @pl.when(elsewhere)
    def _():
        copy = pltpu.make_async_copy(sources[0], out_hbm, sem)
        copy.start()
        copy.wait()


def chosen(value, axis, got, modulus):
    anywhere = pl.BlockSpec(memory_space=pl.ANY)
    return pl.pallas_call(
        functools.partial(chosen_kernel, axis, modulus, tuple(got)),
        in_specs=[anywhere] * (1 + len(got)),
        out_specs=anywhere,
        out_shape=jax.ShapeDtypeStruct(value.shape, value.dtype),
        scratch_shapes=[pltpu.SemaphoreType.DMA],
        compiler_params=pltpu.CompilerParams(vmem_limit_bytes=VMEM_BYTES),
        cost_estimate=cost(0, 2 * value.size),
        name="chosen",
    )(value, *got.values())


def others(value, rows):
    got = [lax.ppermute(value, "row", [(i, (i + k) % rows) for i in range(rows)]) for k in range(1, rows)]
    return got[0] if len(got) == 1 else jnp.concatenate(got, axis=2)


def body(latents, ln_gain, q_weight, k_weight, v_weight, o_weight, gn_gain, conv_weight, conv_bias):
    frames, row_count, cols, ch = latents.shape
    tok = row_count * cols
    size, blocks = lax.axis_size("row"), lax.axis_size("frame")
    pair = size == 2
    x = latents.reshape(frames, tok, ch)

    qt, main, lead, tail, wkp, wvt, wop = project(x, ln_gain, q_weight, k_weight, v_weight, o_weight)
    common = (qt, wkp, wvt)
    routes = [[(f * size + r, (f + 1) * size + (r + k) % size) for f in range(blocks - 1) for r in range(size)]
              for k in range(size)]
    inner = 1
    while inner * inner < blocks:
        inner *= 2
    side = others(main, size)
    prev = lax.ppermute(tail, ("frame", "row"), routes[0])
    spread = fan(lead, "frame", [0], range(inner, blocks, inner))
    first = lead
    state = flash(own_kernel, "own", *common, [first], None, frames - 1, moved=main)

    state, spread = lax.optimization_barrier((state, spread))
    side, tail = lax.optimization_barrier((side, tail))
    came = [lax.ppermute(tail, ("frame", "row"), route) for route in routes[1:]]
    prev_side = came[0] if pair else jnp.concatenate(came, axis=2)
    lead = chosen(lead, "frame", spread, blocks)
    spread = fan(lead, "frame", range(0, blocks, inner), range(1, inner))
    state, mirror = flash(side_kernel, "side", *common, [prev, first], state, frames, moved=side, mirrored=True)

    state, spread = lax.optimization_barrier((state, spread))
    lead = chosen(lead, "frame", spread, inner)
    lead_side = others(lead, size)
    state = flash(lead_kernel, "lead", *common, [prev_side, mirror, lead], state, frames + 1)

    half = frames // 2
    made, into, finished = None, None, []
    for start, count in ((0, half), (half, frames - half)):
        (upd, edge, stats), made = finish(start, count, *common, wop, state, lead_side, made, x, row_count, pair)
        if pair:
            top = bot = lax.ppermute(edge, "row", [(0, 1), (1, 0)])
        else:
            top = lax.ppermute(edge[:, cols:], "row", [(i, i + 1) for i in range(size - 1)])
            bot = lax.ppermute(edge[:, :cols], "row", [(i + 1, i) for i in range(size - 1)])
            stats = lax.psum(stats, "row")
        finished.append((start, upd, top, bot, stats))
    for start, upd, top, bot, stats in finished:
        into = conv(start, frames, upd, top, bot, stats, gn_gain, conv_bias, conv_weight,
                    row_count, pair, tok * size * (ch // GROUPS), into)
    return into[0].reshape(latents.shape)


def solution(mesh):
    in_specs = (P("frame", "row", None, None), P(), P(), P(), P(), P(), P(), P(), P())
    out_specs = P("frame", "row", None, None)
    return jax.shard_map(body, mesh=mesh, in_specs=in_specs, out_specs=out_specs, check_vma=False)
```

profile of v0, /device:TPU:0, one launch (start us, length us, event | category | flops | bytes accessed | tf_op | source)
XLA Modules:
  0.0 83.4 jit_solution(9718756265755707872)
XLA Ops:
  0.0 5.2 %project.1 = (bf16[4,512,512]{2,1,0:T(8,128)(2,1)S(1)}, bf16[3,320,512]{2,1,0:T(8,128)(2,1)}, bf16[1,320,512]{2,1,0:T(8,128)(2,1)S(1)}, bf16[1,320,512]{2,1,0:T(...) custom-call(bf16[4,512,320]{2,1,0:T(8,128)(2,1)} %bitcast.2, ...), custom_call_target="tpu_custom_call" | custom-call | flops 335544320 | bytes 800000 | tf_op jit(solution)/shard_map/project/pallas_call | solution.py:54
  5.2 3.0 %collective-permute-start.4 = (bf16[3,320,512]{2,1,0:T(8,128)(2,1)}, bf16[3,320,512]{2,1,0:T(8,128)(2,1)S(1)}, u32[]{:S(2)}, u32[]{:S(2)}) collective-permute-start(bf16[3,320,512]{2,1,0:T(8,128)(2,1)} %get-tuple-element.39.main_hbm), channel_id=1, source_target_pairs={{0,1},{1,0},{2,3},{3,2},{4,5},{5,4},{6,7},{7,6},{8,9},{9,8},{10,11... | collective-permute-start | bytes 2949128 | tf_op jit(solution)/shard_map/ppermute | solution.py:503
  8.2 5.5 %collective-permute-start.2 = (bf16[1,320,512]{2,1,0:T(8,128)(2,1)S(1)}, bf16[1,320,512]{2,1,0:T(8,128)(2,1)S(1)}, u32[]{:S(2)}, u32[]{:S(2)}) collective-permute-start(bf16[1,320,512]{2,1,0:T(8,128)(2,1)S(1)} %get-tuple-element.38.first_ref.refs_0_), channel_id=1, source_target_pairs={{0,24},{1,25}} | collective-permute-start | bytes 983048 | tf_op jit(solution)/shard_map/ppermute | solution.py:463
  13.8 1.3 %collective-permute-start.1 = (bf16[1,320,512]{2,1,0:T(8,128)(2,1)S(1)}, bf16[1,320,512]{2,1,0:T(8,128)(2,1)S(1)}, u32[]{:S(2)}, u32[]{:S(2)}) collective-permute-start(bf16[1,320,512]{2,1,0:T(8,128)(2,1)S(1)} %get-tuple-element.38.first_ref.refs_0_), channel_id=1, source_target_pairs={{0,16},{1,17}} | collective-permute-start | bytes 983048 | tf_op jit(solution)/shard_map/ppermute | solution.py:463
  15.1 1.3 %collective-permute-start = (bf16[1,320,512]{2,1,0:T(8,128)(2,1)S(1)}, bf16[1,320,512]{2,1,0:T(8,128)(2,1)S(1)}, u32[]{:S(2)}, u32[]{:S(2)}) collective-permute-start(bf16[1,320,512]{2,1,0:T(8,128)(2,1)S(1)} %get-tuple-element.38.first_ref.refs_0_), channel_id=1, source_target_pairs={{0,8},{1,9}} | collective-permute-start | bytes 983048 | tf_op jit(solution)/shard_map/ppermute | solution.py:463
  16.4 1.3 %collective-permute-start.3 = (bf16[1,320,512]{2,1,0:T(8,128)(2,1)S(1)}, bf16[1,320,512]{2,1,0:T(8,128)(2,1)S(1)}, u32[]{:S(2)}, u32[]{:S(2)}) collective-permute-start(bf16[1,320,512]{2,1,0:T(8,128)(2,1)S(1)} %get-tuple-element.50), channel_id=1, source_target_pairs={{0,2},{1,3},{2,4},{3,5},{4,6},{5,7},{6,8},{7,9},{8,10},{9,11},{10,... | collective-permute-start | bytes 983048 | tf_op jit(solution)/shard_map/ppermute | solution.py:522
  17.7 9.2 %own.1.state_in = f32[4,384,512]{2,1,0:T(8,128)} custom-call(bf16[4,512,512]{2,1,0:T(8,128)(2,1)S(1)} %get-tuple-element.34.qt_ref.refs_0_, bf16[320,512]{1,0:T(8,128)(2,1)S(1)} %get-tuple-element.35.wkp_ref.refs_1_, bf16[384,320]{1,0:T(8,128)(2,1)S(1)} %get-tuple-element.36.wvt_ref.refs_2_, bf16[1,320,512]{2,1,0:T(8,128)(2,1)S(1)} %get-tuple-element.38.first_ref.refs_0_, ...), custom_call_target="tpu_custom_call" | custom-call | flops 880803840 | bytes 78643 | tf_op jit(solution)/shard_map/own/pallas_call | solution.py:54
  26.9 0.0 collective-permute-done.2.refs_3_
  26.9 0.0 collective-permute-done.1.refs_2_
  27.0 0.0 collective-permute-done.refs_1_
  27.0 0.1 chosen.2.refs_0_
  27.1 1.3 %collective-permute-start.7 = (bf16[1,320,512]{2,1,0:T(8,128)(2,1)S(1)}, bf16[1,320,512]{2,1,0:T(8,128)(2,1)S(1)}, u32[]{:S(2)}, u32[]{:S(2)}) collective-permute-start(bf16[1,320,512]{2,1,0:T(8,128)(2,1)S(1)} %chosen.2.refs_0_), channel_id=1, source_target_pairs={{0,6},{8,14},{16,22},{24,30},{1,7},{9,15},{17,23},{25,31}} | collective-permute-start | bytes 983048 | tf_op jit(solution)/shard_map/ppermute | solution.py:463
  28.4 1.3 %collective-permute-start.6 = (bf16[1,320,512]{2,1,0:T(8,128)(2,1)S(1)}, bf16[1,320,512]{2,1,0:T(8,128)(2,1)S(1)}, u32[]{:S(2)}, u32[]{:S(2)}) collective-permute-start(bf16[1,320,512]{2,1,0:T(8,128)(2,1)S(1)} %chosen.2.refs_0_), channel_id=1, source_target_pairs={{0,4},{8,12},{16,20},{24,28},{1,5},{9,13},{17,21},{25,29}} | collective-permute-start | bytes 983048 | tf_op jit(solution)/shard_map/ppermute | solution.py:463
  29.8 1.3 %collective-permute-start.5 = (bf16[1,320,512]{2,1,0:T(8,128)(2,1)S(1)}, bf16[1,320,512]{2,1,0:T(8,128)(2,1)S(1)}, u32[]{:S(2)}, u32[]{:S(2)}) collective-permute-start(bf16[1,320,512]{2,1,0:T(8,128)(2,1)S(1)} %chosen.2.refs_0_), channel_id=1, source_target_pairs={{0,2},{8,10},{16,18},{24,26},{1,3},{9,11},{17,19},{25,27}} | collective-permute-start | bytes 983048 | tf_op jit(solution)/shard_map/ppermute | solution.py:463
  31.1 0.0 collective-permute-done.4.side_hbm
  31.1 0.0 copy-start.3
  31.1 1.5 %collective-permute-start.9 = (bf16[1,320,512]{2,1,0:T(8,128)(2,1)S(1)}, bf16[1,320,512]{2,1,0:T(8,128)(2,1)S(1)}, u32[]{:S(2)}, u32[]{:S(2)}) collective-permute-start(bf16[1,320,512]{2,1,0:T(8,128)(2,1)S(1)} %get-tuple-element.50), channel_id=1, source_target_pairs={{0,3},{1,2},{2,5},{3,4},{4,7},{5,6},{6,9},{7,8},{8,11},{9,10},{10,... | collective-permute-start | bytes 983048 | tf_op jit(solution)/shard_map/ppermute | solution.py:529
  32.6 0.0 collective-permute-done.3.prev_ref
  32.6 0.0 copy-done.3
  32.6 11.8 %side.1 = (f32[4,384,512]{2,1,0:T(8,128)}, bf16[1,320,512]{2,1,0:T(8,128)(2,1)S(1)}) custom-call(bf16[4,512,512]{2,1,0:T(8,128)(2,1)S(1)} %get-tuple-element.34.qt_ref.refs_0_, bf16[320,512]{1,0:T(8,128)(2,1)S(1)} %get-tuple-element.35.wkp_ref.refs_1_, bf16[384,320]{1,0:T(8,128)(2,1)S(1)} %get-tuple-element.36.wvt_ref.refs_2_, ...), custom_call_target="tpu_custom_call", output_to_operand_aliasing={{0}: (6, {})} | custom-call | flops 1174405120 | bytes 104857 | tf_op jit(solution)/shard_map/side/pallas_call | solution.py:54
  44.4 0.0 collective-permute-done.7.refs_3_
  44.5 0.0 collective-permute-done.6.refs_2_
  44.5 0.0 collective-permute-done.5.refs_1_
  44.5 0.1 chosen.3.lead_ref
  44.6 0.9 %collective-permute-start.8 = (bf16[1,320,512]{2,1,0:T(8,128)(2,1)S(1)}, bf16[1,320,512]{2,1,0:T(8,128)(2,1)S(1)}, u32[]{:S(2)}, u32[]{:S(2)}) collective-permute-start(bf16[1,320,512]{2,1,0:T(8,128)(2,1)S(1)} %chosen.3.lead_ref), channel_id=1, source_target_pairs={{0,1},{1,0},{2,3},{3,2},{4,5},{5,4},{6,7},{7,6},{8,9},{9,8},{10,11... | collective-permute-start | bytes 983048 | tf_op jit(solution)/shard_map/ppermute | solution.py:503
  45.5 0.0 collective-permute-done.9.prev_ref
  45.6 13.2 %lead.1.refs_5_.refs_6_ = f32[4,384,512]{2,1,0:T(8,128)} custom-call(bf16[4,512,512]{2,1,0:T(8,128)(2,1)S(1)} %get-tuple-element.34.qt_ref.refs_0_, bf16[320,512]{1,0:T(8,128)(2,1)S(1)} %get-tuple-element.35.wkp_ref.refs_1_, bf16[384,320]{1,0:T(8,128)(2,1)S(1)} %get-tuple-element.36.wvt_ref.refs_2_, ...), custom_call_target="tpu_custom_call", output_to_operand_aliasing={{}: (6, {})} | custom-call | flops 1468006400 | bytes 131072 | tf_op jit(solution)/shard_map/lead/pallas_call | solution.py:54
  58.8 0.0 collective-permute-done.8.refs_4_
  58.8 6.7 %finish.2 = (bf16[2,512,320]{2,1,0:T(8,128)(2,1)S(1)}, f32[2,40,320]{2,1,0:T(8,128)S(1)}, f32[2,8,320]{2,1,0:T(8,128)S(1)}, bf16[512,512]{1,0:T(8,128)(2,1)S(1)}, bf16[384,512]{1,0:T(8,128)(2,1)S(1)}) custom-call(bf16[4,512,512]{2,1,0:T(8,128)(2,1)S(1)} %get-tuple-element.34.qt_ref.refs_0_, bf16[320,512]{1,0:T(8,128)(2,1)S(1)} %get-tuple-element.35.wkp_ref.refs_1_, ...), custom_call_target="tpu_custom_call" | custom-call | flops 587202560 | bytes 52428 | tf_op jit(solution)/shard_map/finish/pallas_call | solution.py:54
  65.5 1.2 %collective-permute-start.11 = (f32[2,40,320]{2,1,0:T(8,128)S(1)}, f32[2,40,320]{2,1,0:T(8,128)S(1)}, u32[]{:S(2)}, u32[]{:S(2)}) collective-permute-start(f32[2,40,320]{2,1,0:T(8,128)S(1)} %get-tuple-element.59), channel_id=1, source_target_pairs={{0,1},{1,0},{2,3},{3,2},{4,5},{5,4},{6,7},{7,6},{8,9},{9,8},{10,11... | collective-permute-start | bytes 307208 | tf_op jit(solution)/shard_map/ppermute | solution.py:545
  66.8 0.0 copy-start
  66.8 0.0 copy-start.1
  66.8 0.0 copy-start.2
  66.8 7.1 %finish.3 = (bf16[2,512,320]{2,1,0:T(8,128)(2,1)S(1)}, f32[2,40,320]{2,1,0:T(8,128)S(1)}, f32[2,8,320]{2,1,0:T(8,128)S(1)}) custom-call(bf16[4,512,512]{2,1,0:T(8,128)(2,1)S(1)} %get-tuple-element.34.qt_ref.refs_0_, bf16[320,512]{1,0:T(8,128)(2,1)S(1)} %get-tuple-element.35.wkp_ref.refs_1_, bf16[384,320]{1,0:T(8,128)(2,1)S(1)} %get-tuple-element.36.wvt_ref.refs_2_, ...), custom_call_target="tpu_custom_call" | custom-call | flops 587202560 | bytes 52428 | tf_op jit(solution)/shard_map/finish/pallas_call | solution.py:54
  73.9 0.9 %collective-permute-start.10 = (f32[2,40,320]{2,1,0:T(8,128)S(1)}, f32[2,40,320]{2,1,0:T(8,128)S(1)}, u32[]{:S(2)}, u32[]{:S(2)}) collective-permute-start(f32[2,40,320]{2,1,0:T(8,128)S(1)} %get-tuple-element.56), channel_id=1, source_target_pairs={{0,1},{1,0},{2,3},{3,2},{4,5},{5,4},{6,7},{7,6},{8,9},{9,8},{10,11... | collective-permute-start | bytes 307208 | tf_op jit(solution)/shard_map/ppermute | solution.py:545
  74.8 0.0 collective-permute-done.11.refs_1_.refs_2_
  74.8 0.0 copy-done
  74.8 0.0 copy-done.1
  74.8 0.0 copy-done.2
  74.8 4.0 %conv.2 = (bf16[4,512,320]{2,1,0:T(8,128)(2,1)}, bf16[960,960]{1,0:T(8,128)(2,1)S(1)}) custom-call(bf16[2,512,320]{2,1,0:T(8,128)(2,1)S(1)} %get-tuple-element.58.refs_0_, f32[2,40,320]{2,1,0:T(8,128)S(1)} %collective-permute-done.11.refs_1_.refs_2_, f32[2,40,320]{2,1,0:T(8,128)S(1)} %collective-permute-done.11.refs_1_.refs_2_, ...), custom_call_target="tpu_custom_call" | custom-call | flops 3145728000 | bytes 4000000 | tf_op jit(solution)/shard_map/conv/pallas_call | solution.py:54
  78.9 0.3 collective-permute-done.10.refs_1_.refs_2_
  79.2 4.0 %conv.3 = bf16[4,512,320]{2,1,0:T(8,128)(2,1)} custom-call(bf16[2,512,320]{2,1,0:T(8,128)(2,1)S(1)} %get-tuple-element.55.refs_0_, f32[2,40,320]{2,1,0:T(8,128)S(1)} %collective-permute-done.10.refs_1_.refs_2_, f32[2,40,320]{2,1,0:T(8,128)S(1)} %collective-permute-done.10.refs_1_.refs_2_, ...), custom_call_target="tpu_custom_call", output_to_operand_aliasing={{}: (7, {})} | custom-call | flops 3145728000 | bytes 4000000 | tf_op jit(solution)/shard_map/conv/pallas_call | solution.py:54
Async XLA Ops:
  5.2 25.9 %collective-permute-start.4 = (bf16[3,320,512]{2,1,0:T(8,128)(2,1)}, bf16[3,320,512]{2,1,0:T(8,128)(2,1)S(1)}, u32[]{:S(2)}, u32[]{:S(2)}) collective-permute-start(bf16[3,320,512]{2,1,0:T(8,128)(2,1)} %get-tuple-element.39.main_hbm), channel_id=1, source_target_pairs={{0,1},{1,0},{2,3},{3,2},{4,5},{5,4},{6,7},{7,6},{8,9},{9,8},{10,11... | collective-permute-start | bytes 2949128 | tf_op jit(solution)/shard_map/ppermute | solution.py:503
  8.2 18.7 %collective-permute-start.2 = (bf16[1,320,512]{2,1,0:T(8,128)(2,1)S(1)}, bf16[1,320,512]{2,1,0:T(8,128)(2,1)S(1)}, u32[]{:S(2)}, u32[]{:S(2)}) collective-permute-start(bf16[1,320,512]{2,1,0:T(8,128)(2,1)S(1)} %get-tuple-element.38.first_ref.refs_0_), channel_id=1, source_target_pairs={{0,24},{1,25}} | collective-permute-start | bytes 983048 | tf_op jit(solution)/shard_map/ppermute | solution.py:463
  13.8 13.2 %collective-permute-start.1 = (bf16[1,320,512]{2,1,0:T(8,128)(2,1)S(1)}, bf16[1,320,512]{2,1,0:T(8,128)(2,1)S(1)}, u32[]{:S(2)}, u32[]{:S(2)}) collective-permute-start(bf16[1,320,512]{2,1,0:T(8,128)(2,1)S(1)} %get-tuple-element.38.first_ref.refs_0_), channel_id=1, source_target_pairs={{0,16},{1,17}} | collective-permute-start | bytes 983048 | tf_op jit(solution)/shard_map/ppermute | solution.py:463
  15.1 11.9 %collective-permute-start = (bf16[1,320,512]{2,1,0:T(8,128)(2,1)S(1)}, bf16[1,320,512]{2,1,0:T(8,128)(2,1)S(1)}, u32[]{:S(2)}, u32[]{:S(2)}) collective-permute-start(bf16[1,320,512]{2,1,0:T(8,128)(2,1)S(1)} %get-tuple-element.38.first_ref.refs_0_), channel_id=1, source_target_pairs={{0,8},{1,9}} | collective-permute-start | bytes 983048 | tf_op jit(solution)/shard_map/ppermute | solution.py:463
  16.4 16.2 %collective-permute-start.3 = (bf16[1,320,512]{2,1,0:T(8,128)(2,1)S(1)}, bf16[1,320,512]{2,1,0:T(8,128)(2,1)S(1)}, u32[]{:S(2)}, u32[]{:S(2)}) collective-permute-start(bf16[1,320,512]{2,1,0:T(8,128)(2,1)S(1)} %get-tuple-element.50), channel_id=1, source_target_pairs={{0,2},{1,3},{2,4},{3,5},{4,6},{5,7},{6,8},{7,9},{8,10},{9,11},{10,... | collective-permute-start | bytes 983048 | tf_op jit(solution)/shard_map/ppermute | solution.py:522
  27.1 17.3 %collective-permute-start.7 = (bf16[1,320,512]{2,1,0:T(8,128)(2,1)S(1)}, bf16[1,320,512]{2,1,0:T(8,128)(2,1)S(1)}, u32[]{:S(2)}, u32[]{:S(2)}) collective-permute-start(bf16[1,320,512]{2,1,0:T(8,128)(2,1)S(1)} %chosen.2.refs_0_), channel_id=1, source_target_pairs={{0,6},{8,14},{16,22},{24,30},{1,7},{9,15},{17,23},{25,31}} | collective-permute-start | bytes 983048 | tf_op jit(solution)/shard_map/ppermute | solution.py:463
  28.4 16.0 %collective-permute-start.6 = (bf16[1,320,512]{2,1,0:T(8,128)(2,1)S(1)}, bf16[1,320,512]{2,1,0:T(8,128)(2,1)S(1)}, u32[]{:S(2)}, u32[]{:S(2)}) collective-permute-start(bf16[1,320,512]{2,1,0:T(8,128)(2,1)S(1)} %chosen.2.refs_0_), channel_id=1, source_target_pairs={{0,4},{8,12},{16,20},{24,28},{1,5},{9,13},{17,21},{25,29}} | collective-permute-start | bytes 983048 | tf_op jit(solution)/shard_map/ppermute | solution.py:463
  29.8 14.7 %collective-permute-start.5 = (bf16[1,320,512]{2,1,0:T(8,128)(2,1)S(1)}, bf16[1,320,512]{2,1,0:T(8,128)(2,1)S(1)}, u32[]{:S(2)}, u32[]{:S(2)}) collective-permute-start(bf16[1,320,512]{2,1,0:T(8,128)(2,1)S(1)} %chosen.2.refs_0_), channel_id=1, source_target_pairs={{0,2},{8,10},{16,18},{24,26},{1,3},{9,11},{17,19},{25,27}} | collective-permute-start | bytes 983048 | tf_op jit(solution)/shard_map/ppermute | solution.py:463
  31.1 1.5 %copy-start.3 = (bf16[3,320,512]{2,1,0:T(8,128)(2,1)}, bf16[3,320,512]{2,1,0:T(8,128)(2,1)S(1)}, u32[]{:S(2)}) copy-start(bf16[3,320,512]{2,1,0:T(8,128)(2,1)S(1)} %collective-permute-done.4.side_hbm) | copy-start | bytes 2949124
  31.1 14.5 %collective-permute-start.9 = (bf16[1,320,512]{2,1,0:T(8,128)(2,1)S(1)}, bf16[1,320,512]{2,1,0:T(8,128)(2,1)S(1)}, u32[]{:S(2)}, u32[]{:S(2)}) collective-permute-start(bf16[1,320,512]{2,1,0:T(8,128)(2,1)S(1)} %get-tuple-element.50), channel_id=1, source_target_pairs={{0,3},{1,2},{2,5},{3,4},{4,7},{5,6},{6,9},{7,8},{8,11},{9,10},{10,... | collective-permute-start | bytes 983048 | tf_op jit(solution)/shard_map/ppermute | solution.py:529
  44.6 14.2 %collective-permute-start.8 = (bf16[1,320,512]{2,1,0:T(8,128)(2,1)S(1)}, bf16[1,320,512]{2,1,0:T(8,128)(2,1)S(1)}, u32[]{:S(2)}, u32[]{:S(2)}) collective-permute-start(bf16[1,320,512]{2,1,0:T(8,128)(2,1)S(1)} %chosen.3.lead_ref), channel_id=1, source_target_pairs={{0,1},{1,0},{2,3},{3,2},{4,5},{5,4},{6,7},{7,6},{8,9},{9,8},{10,11... | collective-permute-start | bytes 983048 | tf_op jit(solution)/shard_map/ppermute | solution.py:503
  65.5 9.3 %collective-permute-start.11 = (f32[2,40,320]{2,1,0:T(8,128)S(1)}, f32[2,40,320]{2,1,0:T(8,128)S(1)}, u32[]{:S(2)}, u32[]{:S(2)}) collective-permute-start(f32[2,40,320]{2,1,0:T(8,128)S(1)} %get-tuple-element.59), channel_id=1, source_target_pairs={{0,1},{1,0},{2,3},{3,2},{4,5},{5,4},{6,7},{7,6},{8,9},{9,8},{10,11... | collective-permute-start | bytes 307208 | tf_op jit(solution)/shard_map/ppermute | solution.py:545
  66.8 8.1 %copy-start = (bf16[3,3,320,320]{3,2,1,0:T(8,128)(2,1)S(1)}, bf16[3,3,320,320]{3,2,1,0:T(8,128)(2,1)}, u32[]{:S(2)}) copy-start(bf16[3,3,320,320]{3,2,1,0:T(8,128)(2,1)} %refs_6_.1) | copy-start | bytes 5529604
  66.8 8.1 %copy-start.1 = (bf16[320]{0:T(512)(128)(2,1)S(1)}, bf16[320]{0:T(512)(128)(2,1)}, u32[]{:S(2)}) copy-start(bf16[320]{0:T(512)(128)(2,1)} %refs_4_.3) | copy-start | bytes 1924
  66.8 8.1 %copy-start.2 = (bf16[320]{0:T(512)(128)(2,1)S(1)}, bf16[320]{0:T(512)(128)(2,1)}, u32[]{:S(2)}) copy-start(bf16[320]{0:T(512)(128)(2,1)} %refs_5_.3) | copy-start | bytes 1924
  73.9 5.3 %collective-permute-start.10 = (f32[2,40,320]{2,1,0:T(8,128)S(1)}, f32[2,40,320]{2,1,0:T(8,128)S(1)}, u32[]{:S(2)}, u32[]{:S(2)}) collective-permute-start(f32[2,40,320]{2,1,0:T(8,128)S(1)} %get-tuple-element.56), channel_id=1, source_target_pairs={{0,1},{1,0},{2,3},{3,2},{4,5},{5,4},{6,7},{7,6},{8,9},{9,8},{10,11... | collective-permute-start | bytes 307208 | tf_op jit(solution)/shard_map/ppermute | solution.py:545
where the time goes:
time: 84.3 us; the launch traced here: 83.4 us
  Pallas kernels  61.6 us (73%)
  starting transfers between devices  21 us (25%)
    pallas_call x8, Pallas kernels, kernel_call(): pl.pallas_call(body, in_specs=[in_vmem] * len(near_args) + [anywhere] * l...  61.3 us
    ppermute x6, starting transfers between devices, fan(): got[k] = lax.ppermute(value, axis, route)  12.1 us
    ppermute x2, starting transfers between devices, others(): lax.ppermute(value, 'row', [(i, (i + k) % rows) for i in range(rows)])  3.95 us
    ppermute x2, starting transfers between devices, body(): top = bot = lax.ppermute(edge, 'row', [(0, 1), (1, 0)])  2.17 us
  transfers between devices with their start and end apart: 12, of which 1 were waited for; matrix products, arithmetic and copies ran while one was open for 0% of the time, Pallas kernels for 55%

commit v1 on v0

--- a/solution.py
+++ b/solution.py
@@ -74,30 +74,25 @@
     return jnp.where((inside < dim) & (head * dim + inside == col), 1.0, 0.0).astype(BF16)
 
 
-def project_kernel(x_hbm, g_hbm, wq_hbm, wk_hbm, wv_hbm, wo_hbm,
-                   qt_ref, main_hbm, first_ref, last_ref, wkp_ref, wvt_ref, wop_ref,
-                   x_ref, g_ref, w_ref, main_ref, x_sem, w_sem, main_sem):
+def norm_kernel(x_hbm, g_hbm, wq_hbm, wk_hbm, wv_hbm, wo_hbm, main_hbm, first_ref, last_ref, w_ref,
+                x_ref, g_ref, main_ref, x_sem, g_sem, main_sem, w_sem):
     frames, tok, ch = x_ref.shape
-    copies = [pltpu.make_async_copy(g_hbm, g_ref, w_sem.at[4])]
-    copies += [pltpu.make_async_copy(x_hbm.at[f], x_ref.at[f], x_sem.at[f]) for f in range(frames)]
+    fetch_gain = pltpu.make_async_copy(g_hbm, g_ref, g_sem)
+    fetch_gain.start()
+    copies = [pltpu.make_async_copy(x_hbm.at[f], x_ref.at[f], x_sem.at[f]) for f in range(frames)]
     weights = [pltpu.make_async_copy(w, w_ref.at[k], w_sem.at[k])
                for k, w in enumerate((wq_hbm, wk_hbm, wv_hbm, wo_hbm))]
     for copy in copies + weights:
         copy.start()
-    ek, ev = head_spread(ch, KPAD), head_spread(ch, VPAD)
-    copies[0].wait()
+    fetch_gain.wait()
     gain = jnp.broadcast_to(g_ref[...].astype(F32).reshape(1, ch), (8, ch)).T[:, 0:1]
-
-    def normed(f):
-        copies[1 + f].wait()
+    leave = []
+    for f in range(frames):
+        copies[f].wait()
         floated = x_ref[f].astype(F32).T
         centre = floated - jnp.sum(floated, axis=0, keepdims=True) / ch
         spread = jnp.sum(centre * centre, axis=0, keepdims=True) / ch
-        return (centre * lax.rsqrt(spread + 1e-05) * gain).astype(BF16)
-
-    leave = []
-    for f in range(frames):
-        value = normed(f)
+        value = (centre * lax.rsqrt(spread + 1e-05) * gain).astype(BF16)
         if f < frames - 1:
             main_ref[f] = value
             leave.append(pltpu.make_async_copy(main_ref.at[f], main_hbm.at[f], main_sem.at[f]))
@@ -106,26 +101,43 @@
             last_ref[0] = value
         if f == 0:
             first_ref[0] = value
-            for copy in weights:
-                copy.wait()
-            wqt = nt(ek, w_ref[0]).astype(BF16)
-            wkp_ref[...] = nt(w_ref[1], ek).astype(BF16)
-            wvt_ref[...] = nt(ev, w_ref[2]).astype(BF16)
-            wop_ref[...] = dot(ev, w_ref[3]).astype(BF16)
+    for copy in leave + weights:
+        copy.wait()
+
+
+def norm(x, gain, wq, wk, wv, wo):
+    frames, tok, ch = x.shape
+    outs = [far_of(frames - 1, ch, tok), near_of(1, ch, tok), near_of(1, ch, tok), near_of(4, ch, ch)]
+    scratch = [pltpu.VMEM(x.shape, BF16), pltpu.VMEM((ch,), BF16), pltpu.VMEM((frames - 1, ch, tok), BF16),
+               pltpu.SemaphoreType.DMA((frames,)), pltpu.SemaphoreType.DMA, pltpu.SemaphoreType.DMA((frames - 1,)),
+               pltpu.SemaphoreType.DMA((4,))]
+    return kernel_call(norm_kernel, "norm", [], [x, gain, wq, wk, wv, wo], outs, scratch, cost(frames * tok * ch * 20, 4e5))
+
+
+def project_kernel(first_ref, last_ref, w_ref, main_hbm,
+                   qt_ref, wkp_ref, wvt_ref, wop_ref, main_ref, main_sem):
+    frames, ch = qt_ref.shape[0], first_ref.shape[1]
+    blocks = [pltpu.make_async_copy(main_hbm.at[f], main_ref.at[f], main_sem.at[f]) for f in range(1, frames - 1)]
+    for copy in blocks:
+        copy.start()
+    ek, ev = head_spread(ch, KPAD), head_spread(ch, VPAD)
+    wqt = nt(ek, w_ref[0]).astype(BF16)
+    wkp_ref[...] = nt(w_ref[1], ek).astype(BF16)
+    wvt_ref[...] = nt(ev, w_ref[2]).astype(BF16)
+    wop_ref[...] = dot(ev, w_ref[3]).astype(BF16)
+    for copy in blocks:
+        copy.wait()
+    for f in range(frames):
+        value = first_ref[0] if f == 0 else last_ref[0] if f == frames - 1 else main_ref[f]
         qt_ref[f] = dot(wqt, value).astype(BF16)
-    for copy in leave:
-        copy.wait()
-
-
-def project(x, gain, wq, wk, wv, wo):
-    frames, tok, ch = x.shape
-    nk, nv = HEADS * KPAD, HEADS * VPAD
-    outs = [near_of(frames, nk, tok), far_of(frames - 1, ch, tok), near_of(1, ch, tok), near_of(1, ch, tok),
-            near_of(ch, nk), near_of(nv, ch), near_of(nv, ch)]
-    scratch = [pltpu.VMEM(x.shape, BF16), pltpu.VMEM((ch,), BF16), pltpu.VMEM((4, ch, ch), BF16),
-               pltpu.VMEM((frames - 1, ch, tok), BF16), pltpu.SemaphoreType.DMA((frames,)),
-               pltpu.SemaphoreType.DMA((5,)), pltpu.SemaphoreType.DMA((frames - 1,))]
-    return kernel_call(project_kernel, "project", [], [x, gain, wq, wk, wv, wo], outs, scratch,
+
+
+def project(main, first, last, weights):
+    ch, tok = main.shape[1:]
+    frames, nk, nv = main.shape[0] + 1, HEADS * KPAD, HEADS * VPAD
+    outs = [near_of(frames, nk, tok), near_of(ch, nk), near_of(nv, ch), near_of(nv, ch)]
+    scratch = [pltpu.VMEM(main.shape, BF16), pltpu.SemaphoreType.DMA((frames - 1,))]
+    return kernel_call(project_kernel, "project", [first, last, weights], [main], outs, scratch,
                        cost(frames * tok * ch * nk, 8e5))
 
 
@@ -511,7 +523,8 @@
     pair = size == 2
     x = latents.reshape(frames, tok, ch)
 
-    qt, main, lead, tail, wkp, wvt, wop = project(x, ln_gain, q_weight, k_weight, v_weight, o_weight)
+    main, lead, tail, weights = norm(x, ln_gain, q_weight, k_weight, v_weight, o_weight)
+    qt, wkp, wvt, wop = project(main, lead, tail, weights)
     common = (qt, wkp, wvt)
     routes = [[(f * size + r, (f + 1) * size + (r + k) % size) for f in range(blocks - 1) for r in range(size)]
               for k in range(size)]

time: 84.3 us -> 83.9 us (level)
    pallas_call x8 -> x9, Pallas kernels: 61.3 us -> 61.8 us  [kernel_call(): pl.pallas_call(body, in_specs=[in_vmem] * len(near_args) + [anywhere] * l...]
  transfers between devices with their start and end apart: 12 -> 12, of which waited for: 1 -> 1; matrix products, arithmetic and copies ran while one was open for 0% -> 0% of each run, Pallas kernels for 55% -> 57%
where the time goes in v1:
time: 83.9 us; the launch traced here: 83.5 us
  Pallas kernels  62.1 us (74%)
  starting transfers between devices  20.6 us (25%)
    pallas_call x9, Pallas kernels, kernel_call(): pl.pallas_call(body, in_specs=[in_vmem] * len(near_args) + [anywhere] * l...  61.8 us
    ppermute x6, starting transfers between devices, fan(): got[k] = lax.ppermute(value, axis, route)  12.1 us
    ppermute x2, starting transfers between devices, others(): lax.ppermute(value, 'row', [(i, (i + k) % rows) for i in range(rows)])  3.6 us
    ppermute x2, starting transfers between devices, body(): top = bot = lax.ppermute(edge, 'row', [(0, 1), (1, 0)])  2.17 us
  transfers between devices with their start and end apart: 12, of which 1 were waited for; matrix products, arithmetic and copies ran while one was open for 0% of the time, Pallas kernels for 57%

profile of v1, /device:TPU:0, one launch (start us, length us, event | category | flops | bytes accessed | tf_op | source)
XLA Modules:
  0.0 83.5 jit_solution(8078807235928311751)
XLA Ops:
  0.0 3.4 %norm.1 = (bf16[3,320,512]{2,1,0:T(8,128)(2,1)}, bf16[1,320,512]{2,1,0:T(8,128)(2,1)S(1)}, bf16[1,320,512]{2,1,0:T(8,128)(2,1)S(1)}, bf16[4,320,320]{2,1,0:T(8,128)(2,1)S(1)}) custom-call(bf16[4,512,320]{2,1,0:T(8,128)(2,1)} %bitcast.2, bf16[320]{0:T(512)(128)(2,1)} %g_hbm.1, bf16[320,320]{1,0:T(8,128)(2,1)} %wq_hbm.1, bf16[320,320]{1,0:T(8,128)(2,1)} %wk_hbm.1, ...), custom_call_target="tpu_custom_call" | custom-call | flops 13107200 | bytes 400000 | tf_op jit(solution)/shard_map/norm/pallas_call | solution.py:54
  3.4 3.0 %collective-permute-start.4 = (bf16[3,320,512]{2,1,0:T(8,128)(2,1)}, bf16[3,320,512]{2,1,0:T(8,128)(2,1)S(1)}, u32[]{:S(2)}, u32[]{:S(2)}) collective-permute-start(bf16[3,320,512]{2,1,0:T(8,128)(2,1)} %get-tuple-element.38.main_hbm), channel_id=1, source_target_pairs={{0,1},{1,0},{2,3},{3,2},{4,5},{5,4},{6,7},{7,6},{8,9},{9,8},{10,11... | collective-permute-start | bytes 2949128 | tf_op jit(solution)/shard_map/ppermute | solution.py:515
  6.4 5.5 %collective-permute-start.2 = (bf16[1,320,512]{2,1,0:T(8,128)(2,1)S(1)}, bf16[1,320,512]{2,1,0:T(8,128)(2,1)S(1)}, u32[]{:S(2)}, u32[]{:S(2)}) collective-permute-start(bf16[1,320,512]{2,1,0:T(8,128)(2,1)S(1)} %get-tuple-element.35.first_ref.refs_0_), channel_id=1, source_target_pairs={{0,24},{1,25}} | collective-permute-start | bytes 983048 | tf_op jit(solution)/shard_map/ppermute | solution.py:475
  11.9 1.3 %collective-permute-start.1 = (bf16[1,320,512]{2,1,0:T(8,128)(2,1)S(1)}, bf16[1,320,512]{2,1,0:T(8,128)(2,1)S(1)}, u32[]{:S(2)}, u32[]{:S(2)}) collective-permute-start(bf16[1,320,512]{2,1,0:T(8,128)(2,1)S(1)} %get-tuple-element.35.first_ref.refs_0_), channel_id=1, source_target_pairs={{0,16},{1,17}} | collective-permute-start | bytes 983048 | tf_op jit(solution)/shard_map/ppermute | solution.py:475
  13.3 1.3 %collective-permute-start = (bf16[1,320,512]{2,1,0:T(8,128)(2,1)S(1)}, bf16[1,320,512]{2,1,0:T(8,128)(2,1)S(1)}, u32[]{:S(2)}, u32[]{:S(2)}) collective-permute-start(bf16[1,320,512]{2,1,0:T(8,128)(2,1)S(1)} %get-tuple-element.35.first_ref.refs_0_), channel_id=1, source_target_pairs={{0,8},{1,9}} | collective-permute-start | bytes 983048 | tf_op jit(solution)/shard_map/ppermute | solution.py:475
  14.6 1.3 %collective-permute-start.3 = (bf16[1,320,512]{2,1,0:T(8,128)(2,1)S(1)}, bf16[1,320,512]{2,1,0:T(8,128)(2,1)S(1)}, u32[]{:S(2)}, u32[]{:S(2)}) collective-permute-start(bf16[1,320,512]{2,1,0:T(8,128)(2,1)S(1)} %get-tuple-element.52.last_ref), channel_id=1, source_target_pairs={{0,2},{1,3},{2,4},{3,5},{4,6},{5,7},{6,8},{7,9},{8,10},{9,11},{10,... | collective-permute-start | bytes 983048 | tf_op jit(solution)/shard_map/ppermute | solution.py:535
  15.9 2.4 %project.1 = (bf16[4,512,512]{2,1,0:T(8,128)(2,1)S(1)}, bf16[320,512]{1,0:T(8,128)(2,1)S(1)}, bf16[384,320]{1,0:T(8,128)(2,1)S(1)}, bf16[384,320]{1,0:T(8,128)(2,1)S(1)}) custom-call(bf16[1,320,512]{2,1,0:T(8,128)(2,1)S(1)} %get-tuple-element.35.first_ref.refs_0_, bf16[1,320,512]{2,1,0:T(8,128)(2,1)S(1)} %get-tuple-element.52.last_ref, ...), custom_call_target="tpu_custom_call" | custom-call | flops 335544320 | bytes 800000 | tf_op jit(solution)/shard_map/project/pallas_call | solution.py:54
  18.3 9.2 %own.1.state_in = f32[4,384,512]{2,1,0:T(8,128)} custom-call(bf16[4,512,512]{2,1,0:T(8,128)(2,1)S(1)} %get-tuple-element.39.qt_ref.refs_0_, bf16[320,512]{1,0:T(8,128)(2,1)S(1)} %get-tuple-element.40.wkp_ref.refs_1_, bf16[384,320]{1,0:T(8,128)(2,1)S(1)} %get-tuple-element.41.wvt_ref.refs_2_, bf16[1,320,512]{2,1,0:T(8,128)(2,1)S(1)} %get-tuple-element.35.first_ref.refs_0_, ...), custom_call_target="tpu_custom_call" | custom-call | flops 880803840 | bytes 78643 | tf_op jit(solution)/shard_map/own/pallas_call | solution.py:54
  27.5 0.0 collective-permute-done.2.refs_3_
  27.5 0.0 collective-permute-done.1.refs_2_
  27.5 0.0 collective-permute-done.refs_1_
  27.5 0.1 chosen.2.refs_0_
  27.7 1.3 %collective-permute-start.7 = (bf16[1,320,512]{2,1,0:T(8,128)(2,1)S(1)}, bf16[1,320,512]{2,1,0:T(8,128)(2,1)S(1)}, u32[]{:S(2)}, u32[]{:S(2)}) collective-permute-start(bf16[1,320,512]{2,1,0:T(8,128)(2,1)S(1)} %chosen.2.refs_0_), channel_id=1, source_target_pairs={{0,6},{8,14},{16,22},{24,30},{1,7},{9,15},{17,23},{25,31}} | collective-permute-start | bytes 983048 | tf_op jit(solution)/shard_map/ppermute | solution.py:475
  29.0 1.3 %collective-permute-start.6 = (bf16[1,320,512]{2,1,0:T(8,128)(2,1)S(1)}, bf16[1,320,512]{2,1,0:T(8,128)(2,1)S(1)}, u32[]{:S(2)}, u32[]{:S(2)}) collective-permute-start(bf16[1,320,512]{2,1,0:T(8,128)(2,1)S(1)} %chosen.2.refs_0_), channel_id=1, source_target_pairs={{0,4},{8,12},{16,20},{24,28},{1,5},{9,13},{17,21},{25,29}} | collective-permute-start | bytes 983048 | tf_op jit(solution)/shard_map/ppermute | solution.py:475
  30.3 1.3 %collective-permute-start.5 = (bf16[1,320,512]{2,1,0:T(8,128)(2,1)S(1)}, bf16[1,320,512]{2,1,0:T(8,128)(2,1)S(1)}, u32[]{:S(2)}, u32[]{:S(2)}) collective-permute-start(bf16[1,320,512]{2,1,0:T(8,128)(2,1)S(1)} %chosen.2.refs_0_), channel_id=1, source_target_pairs={{0,2},{8,10},{16,18},{24,26},{1,3},{9,11},{17,19},{25,27}} | collective-permute-start | bytes 983048 | tf_op jit(solution)/shard_map/ppermute | solution.py:475
  31.6 0.0 collective-permute-done.4.side_hbm
  31.6 0.0 copy-start.3
  31.6 1.5 %collective-permute-start.9 = (bf16[1,320,512]{2,1,0:T(8,128)(2,1)S(1)}, bf16[1,320,512]{2,1,0:T(8,128)(2,1)S(1)}, u32[]{:S(2)}, u32[]{:S(2)}) collective-permute-start(bf16[1,320,512]{2,1,0:T(8,128)(2,1)S(1)} %get-tuple-element.52.last_ref), channel_id=1, source_target_pairs={{0,3},{1,2},{2,5},{3,4},{4,7},{5,6},{6,9},{7,8},{8,11},{9,10},{10,... | collective-permute-start | bytes 983048 | tf_op jit(solution)/shard_map/ppermute | solution.py:542
  33.1 0.0 collective-permute-done.3.prev_ref
  33.1 0.0 copy-done.3
  33.2 11.8 %side.1 = (f32[4,384,512]{2,1,0:T(8,128)}, bf16[1,320,512]{2,1,0:T(8,128)(2,1)S(1)}) custom-call(bf16[4,512,512]{2,1,0:T(8,128)(2,1)S(1)} %get-tuple-element.39.qt_ref.refs_0_, bf16[320,512]{1,0:T(8,128)(2,1)S(1)} %get-tuple-element.40.wkp_ref.refs_1_, bf16[384,320]{1,0:T(8,128)(2,1)S(1)} %get-tuple-element.41.wvt_ref.refs_2_, ...), custom_call_target="tpu_custom_call", output_to_operand_aliasing={{0}: (6, {})} | custom-call | flops 1174405120 | bytes 104857 | tf_op jit(solution)/shard_map/side/pallas_call | solution.py:54
  45.0 0.0 collective-permute-done.7.refs_3_
  45.0 0.0 collective-permute-done.6.refs_2_
  45.0 0.0 collective-permute-done.5.refs_1_
  45.0 0.1 chosen.3.lead_ref
  45.2 0.6 collective-permute-start.8
  45.7 0.0 collective-permute-done.9.prev_ref
  45.7 13.2 %lead.1.refs_5_.refs_6_ = f32[4,384,512]{2,1,0:T(8,128)} custom-call(bf16[4,512,512]{2,1,0:T(8,128)(2,1)S(1)} %get-tuple-element.39.qt_ref.refs_0_, bf16[320,512]{1,0:T(8,128)(2,1)S(1)} %get-tuple-element.40.wkp_ref.refs_1_, bf16[384,320]{1,0:T(8,128)(2,1)S(1)} %get-tuple-element.41.wvt_ref.refs_2_, ...), custom_call_target="tpu_custom_call", output_to_operand_aliasing={{}: (6, {})} | custom-call | flops 1468006400 | bytes 131072 | tf_op jit(solution)/shard_map/lead/pallas_call | solution.py:54
  59.0 0.0 collective-permute-done.8.refs_4_
  59.0 6.7 %finish.2 = (bf16[2,512,320]{2,1,0:T(8,128)(2,1)S(1)}, f32[2,40,320]{2,1,0:T(8,128)S(1)}, f32[2,8,320]{2,1,0:T(8,128)S(1)}, bf16[512,512]{1,0:T(8,128)(2,1)S(1)}, bf16[384,512]{1,0:T(8,128)(2,1)S(1)}) custom-call(bf16[4,512,512]{2,1,0:T(8,128)(2,1)S(1)} %get-tuple-element.39.qt_ref.refs_0_, bf16[320,512]{1,0:T(8,128)(2,1)S(1)} %get-tuple-element.40.wkp_ref.refs_1_, ...), custom_call_target="tpu_custom_call" | custom-call | flops 587202560 | bytes 52428 | tf_op jit(solution)/shard_map/finish/pallas_call | solution.py:54
  65.7 1.6 %collective-permute-start.11 = (f32[2,40,320]{2,1,0:T(8,128)S(1)}, f32[2,40,320]{2,1,0:T(8,128)S(1)}, u32[]{:S(2)}, u32[]{:S(2)}) collective-permute-start(f32[2,40,320]{2,1,0:T(8,128)S(1)} %get-tuple-element.61), channel_id=1, source_target_pairs={{0,1},{1,0},{2,3},{3,2},{4,5},{5,4},{6,7},{7,6},{8,9},{9,8},{10,11... | collective-permute-start | bytes 307208 | tf_op jit(solution)/shard_map/ppermute | solution.py:558
  67.3 0.0 copy-start
  67.3 0.0 copy-start.1
  67.3 0.0 copy-start.2
  67.3 7.1 %finish.3 = (bf16[2,512,320]{2,1,0:T(8,128)(2,1)S(1)}, f32[2,40,320]{2,1,0:T(8,128)S(1)}, f32[2,8,320]{2,1,0:T(8,128)S(1)}) custom-call(bf16[4,512,512]{2,1,0:T(8,128)(2,1)S(1)} %get-tuple-element.39.qt_ref.refs_0_, bf16[320,512]{1,0:T(8,128)(2,1)S(1)} %get-tuple-element.40.wkp_ref.refs_1_, bf16[384,320]{1,0:T(8,128)(2,1)S(1)} %get-tuple-element.41.wvt_ref.refs_2_, ...), custom_call_target="tpu_custom_call" | custom-call | flops 587202560 | bytes 52428 | tf_op jit(solution)/shard_map/finish/pallas_call | solution.py:54
  74.4 0.6 collective-permute-start.10
  75.0 0.0 collective-permute-done.11.refs_1_.refs_2_
  75.0 0.0 copy-done
  75.0 0.0 copy-done.1
  75.0 0.0 copy-done.2
  75.0 4.0 %conv.2 = (bf16[4,512,320]{2,1,0:T(8,128)(2,1)}, bf16[960,960]{1,0:T(8,128)(2,1)S(1)}) custom-call(bf16[2,512,320]{2,1,0:T(8,128)(2,1)S(1)} %get-tuple-element.60.refs_0_, f32[2,40,320]{2,1,0:T(8,128)S(1)} %collective-permute-done.11.refs_1_.refs_2_, f32[2,40,320]{2,1,0:T(8,128)S(1)} %collective-permute-done.11.refs_1_.refs_2_, ...), custom_call_target="tpu_custom_call" | custom-call | flops 3145728000 | bytes 4000000 | tf_op jit(solution)/shard_map/conv/pallas_call | solution.py:54
  79.0 0.3 collective-permute-done.10.refs_1_.refs_2_
  79.4 4.0 %conv.3 = bf16[4,512,320]{2,1,0:T(8,128)(2,1)} custom-call(bf16[2,512,320]{2,1,0:T(8,128)(2,1)S(1)} %get-tuple-element.57.refs_0_, f32[2,40,320]{2,1,0:T(8,128)S(1)} %collective-permute-done.10.refs_1_.refs_2_, f32[2,40,320]{2,1,0:T(8,128)S(1)} %collective-permute-done.10.refs_1_.refs_2_, ...), custom_call_target="tpu_custom_call", output_to_operand_aliasing={{}: (7, {})} | custom-call | flops 3145728000 | bytes 4000000 | tf_op jit(solution)/shard_map/conv/pallas_call | solution.py:54
Async XLA Ops:
  3.4 28.2 %collective-permute-start.4 = (bf16[3,320,512]{2,1,0:T(8,128)(2,1)}, bf16[3,320,512]{2,1,0:T(8,128)(2,1)S(1)}, u32[]{:S(2)}, u32[]{:S(2)}) collective-permute-start(bf16[3,320,512]{2,1,0:T(8,128)(2,1)} %get-tuple-element.38.main_hbm), channel_id=1, source_target_pairs={{0,1},{1,0},{2,3},{3,2},{4,5},{5,4},{6,7},{7,6},{8,9},{9,8},{10,11... | collective-permute-start | bytes 2949128 | tf_op jit(solution)/shard_map/ppermute | solution.py:515
  6.4 21.1 %collective-permute-start.2 = (bf16[1,320,512]{2,1,0:T(8,128)(2,1)S(1)}, bf16[1,320,512]{2,1,0:T(8,128)(2,1)S(1)}, u32[]{:S(2)}, u32[]{:S(2)}) collective-permute-start(bf16[1,320,512]{2,1,0:T(8,128)(2,1)S(1)} %get-tuple-element.35.first_ref.refs_0_), channel_id=1, source_target_pairs={{0,24},{1,25}} | collective-permute-start | bytes 983048 | tf_op jit(solution)/shard_map/ppermute | solution.py:475
  11.9 15.5 %collective-permute-start.1 = (bf16[1,320,512]{2,1,0:T(8,128)(2,1)S(1)}, bf16[1,320,512]{2,1,0:T(8,128)(2,1)S(1)}, u32[]{:S(2)}, u32[]{:S(2)}) collective-permute-start(bf16[1,320,512]{2,1,0:T(8,128)(2,1)S(1)} %get-tuple-element.35.first_ref.refs_0_), channel_id=1, source_target_pairs={{0,16},{1,17}} | collective-permute-start | bytes 983048 | tf_op jit(solution)/shard_map/ppermute | solution.py:475
  13.3 14.2 %collective-permute-start = (bf16[1,320,512]{2,1,0:T(8,128)(2,1)S(1)}, bf16[1,320,512]{2,1,0:T(8,128)(2,1)S(1)}, u32[]{:S(2)}, u32[]{:S(2)}) collective-permute-start(bf16[1,320,512]{2,1,0:T(8,128)(2,1)S(1)} %get-tuple-element.35.first_ref.refs_0_), channel_id=1, source_target_pairs={{0,8},{1,9}} | collective-permute-start | bytes 983048 | tf_op jit(solution)/shard_map/ppermute | solution.py:475
  14.6 18.6 %collective-permute-start.3 = (bf16[1,320,512]{2,1,0:T(8,128)(2,1)S(1)}, bf16[1,320,512]{2,1,0:T(8,128)(2,1)S(1)}, u32[]{:S(2)}, u32[]{:S(2)}) collective-permute-start(bf16[1,320,512]{2,1,0:T(8,128)(2,1)S(1)} %get-tuple-element.52.last_ref), channel_id=1, source_target_pairs={{0,2},{1,3},{2,4},{3,5},{4,6},{5,7},{6,8},{7,9},{8,10},{9,11},{10,... | collective-permute-start | bytes 983048 | tf_op jit(solution)/shard_map/ppermute | solution.py:535
  27.7 17.3 %collective-permute-start.7 = (bf16[1,320,512]{2,1,0:T(8,128)(2,1)S(1)}, bf16[1,320,512]{2,1,0:T(8,128)(2,1)S(1)}, u32[]{:S(2)}, u32[]{:S(2)}) collective-permute-start(bf16[1,320,512]{2,1,0:T(8,128)(2,1)S(1)} %chosen.2.refs_0_), channel_id=1, source_target_pairs={{0,6},{8,14},{16,22},{24,30},{1,7},{9,15},{17,23},{25,31}} | collective-permute-start | bytes 983048 | tf_op jit(solution)/shard_map/ppermute | solution.py:475
  29.0 16.0 %collective-permute-start.6 = (bf16[1,320,512]{2,1,0:T(8,128)(2,1)S(1)}, bf16[1,320,512]{2,1,0:T(8,128)(2,1)S(1)}, u32[]{:S(2)}, u32[]{:S(2)}) collective-permute-start(bf16[1,320,512]{2,1,0:T(8,128)(2,1)S(1)} %chosen.2.refs_0_), channel_id=1, source_target_pairs={{0,4},{8,12},{16,20},{24,28},{1,5},{9,13},{17,21},{25,29}} | collective-permute-start | bytes 983048 | tf_op jit(solution)/shard_map/ppermute | solution.py:475
  30.3 14.7 %collective-permute-start.5 = (bf16[1,320,512]{2,1,0:T(8,128)(2,1)S(1)}, bf16[1,320,512]{2,1,0:T(8,128)(2,1)S(1)}, u32[]{:S(2)}, u32[]{:S(2)}) collective-permute-start(bf16[1,320,512]{2,1,0:T(8,128)(2,1)S(1)} %chosen.2.refs_0_), channel_id=1, source_target_pairs={{0,2},{8,10},{16,18},{24,26},{1,3},{9,11},{17,19},{25,27}} | collective-permute-start | bytes 983048 | tf_op jit(solution)/shard_map/ppermute | solution.py:475
  31.6 1.5 %copy-start.3 = (bf16[3,320,512]{2,1,0:T(8,128)(2,1)}, bf16[3,320,512]{2,1,0:T(8,128)(2,1)S(1)}, u32[]{:S(2)}) copy-start(bf16[3,320,512]{2,1,0:T(8,128)(2,1)S(1)} %collective-permute-done.4.side_hbm) | copy-start | bytes 2949124
  31.6 14.1 %collective-permute-start.9 = (bf16[1,320,512]{2,1,0:T(8,128)(2,1)S(1)}, bf16[1,320,512]{2,1,0:T(8,128)(2,1)S(1)}, u32[]{:S(2)}, u32[]{:S(2)}) collective-permute-start(bf16[1,320,512]{2,1,0:T(8,128)(2,1)S(1)} %get-tuple-element.52.last_ref), channel_id=1, source_target_pairs={{0,3},{1,2},{2,5},{3,4},{4,7},{5,6},{6,9},{7,8},{8,11},{9,10},{10,... | collective-permute-start | bytes 983048 | tf_op jit(solution)/shard_map/ppermute | solution.py:542
  45.2 13.8 %collective-permute-start.8 = (bf16[1,320,512]{2,1,0:T(8,128)(2,1)S(1)}, bf16[1,320,512]{2,1,0:T(8,128)(2,1)S(1)}, u32[]{:S(2)}, u32[]{:S(2)}) collective-permute-start(bf16[1,320,512]{2,1,0:T(8,128)(2,1)S(1)} %chosen.3.lead_ref), channel_id=1, source_target_pairs={{0,1},{1,0},{2,3},{3,2},{4,5},{5,4},{6,7},{7,6},{8,9},{9,8},{10,11... | collective-permute-start | bytes 983048 | tf_op jit(solution)/shard_map/ppermute | solution.py:515
  65.7 9.3 %collective-permute-start.11 = (f32[2,40,320]{2,1,0:T(8,128)S(1)}, f32[2,40,320]{2,1,0:T(8,128)S(1)}, u32[]{:S(2)}, u32[]{:S(2)}) collective-permute-start(f32[2,40,320]{2,1,0:T(8,128)S(1)} %get-tuple-element.61), channel_id=1, source_target_pairs={{0,1},{1,0},{2,3},{3,2},{4,5},{5,4},{6,7},{7,6},{8,9},{9,8},{10,11... | collective-permute-start | bytes 307208 | tf_op jit(solution)/shard_map/ppermute | solution.py:558
  67.3 7.7 %copy-start = (bf16[3,3,320,320]{3,2,1,0:T(8,128)(2,1)S(1)}, bf16[3,3,320,320]{3,2,1,0:T(8,128)(2,1)}, u32[]{:S(2)}) copy-start(bf16[3,3,320,320]{3,2,1,0:T(8,128)(2,1)} %refs_6_.1) | copy-start | bytes 5529604
  67.3 7.7 %copy-start.1 = (bf16[320]{0:T(512)(128)(2,1)S(1)}, bf16[320]{0:T(512)(128)(2,1)}, u32[]{:S(2)}) copy-start(bf16[320]{0:T(512)(128)(2,1)} %refs_4_.3) | copy-start | bytes 1924
  67.3 7.7 %copy-start.2 = (bf16[320]{0:T(512)(128)(2,1)S(1)}, bf16[320]{0:T(512)(128)(2,1)}, u32[]{:S(2)}) copy-start(bf16[320]{0:T(512)(128)(2,1)} %refs_5_.3) | copy-start | bytes 1924
  74.4 4.9 %collective-permute-start.10 = (f32[2,40,320]{2,1,0:T(8,128)S(1)}, f32[2,40,320]{2,1,0:T(8,128)S(1)}, u32[]{:S(2)}, u32[]{:S(2)}) collective-permute-start(f32[2,40,320]{2,1,0:T(8,128)S(1)} %get-tuple-element.58), channel_id=1, source_target_pairs={{0,1},{1,0},{2,3},{3,2},{4,5},{5,4},{6,7},{7,6},{8,9},{9,8},{10,11... | collective-permute-start | bytes 307208 | tf_op jit(solution)/shard_map/ppermute | solution.py:558
